TPU v7x, 32 devices: a whole 2x2x4 slice. The times are simulated.
32 devices in a mesh: groups: 2 (over y), expert: 4 (over z), node: 2 (over x), inner: 2 (over core).
Axes of the slice: x: 2, y: 2, z: 4, core: 2. Of those that a mesh axis runs over, the one named last changes fastest.
Arguments:
- tokens: bfloat16 [2048, 2048], P(('groups', 'expert', 'node', 'inner')), parts along dimension 0, may hold values from -6 to 6
- slot_choice: int32 [2048, 8], P(('groups', 'expert', 'node', 'inner')), parts along dimension 0, may hold values from 0 to 15, all different within a row; in each aligned block of 64 rows (0 to 63, 64 to 127, ...) at most 64 rows name the same one
- gate_fixed: int32 [2048, 8], P(('groups', 'expert', 'node', 'inner')), parts along dimension 0, may hold values from 1 to 65536
- expert_gate: bfloat16 [8, 2048, 384], P(('expert', 'node')), may hold values from -0.125 to 0.125
- expert_up: bfloat16 [8, 2048, 384], P(('expert', 'node')), may hold values from -0.125 to 0.125
- expert_down: bfloat16 [8, 384, 2048], P(('expert', 'node')), may hold values from -0.3125 to 0.3125
- next_weights: bfloat16 [8, 3, 2048, 384], P(('expert', 'node'), None, 'inner'), may hold values from -6 to 6
- hot_expert: int32 [4], P('groups'), parts along dimension 0, may hold values from 0 to 7, as said below
- slot_take: int32 [32], P(('groups', 'expert', 'node', 'inner')), parts along dimension 0, may hold values from 0 to 2
Outputs:
- moe_out: bfloat16 [2048, 2048], P(('groups', 'expert', 'node', 'inner')), parts along dimension 0
- new_weights: bfloat16 [32, 3, 2048, 384], P(('groups', 'expert', 'node', 'inner')), parts along dimension 0
There are 2 independent parts, one for each index of `groups`. A program takes and returns all parts, laid end to end along the dimension named above; an argument that names none is the same for every part. Nothing has to cross between parts.
Inputs may be any that keep to these rules, and one draw needn't show every extreme that they name: `slot_choice`: a token's 8 slots differ; at most 64 of the pairs of one device's tokens name one slot, and in every draw some device names some slot exactly 64 times. `hot_expert`: the 2 entries are different experts; expert 8 - 1 is always one of them.
All inputs are finite; a program needn't handle non-finite values.
Results may differ from a plain program's by a relative error of at most 0.0058.
Values may be sent and summed in bfloat16 or wider, within the bound.
A program may use at most 128 MiB of HBM per device.

v0:
```python
import jax
import jax.numpy as jnp
from jax import lax
from jax.sharding import PartitionSpec as P


def spread(block, axis, owner):
    block = jnp.where(lax.axis_index(axis) == owner, block, jnp.zeros_like(block))
    return lax.psum(block, axis)


def shards(
    tokens,
    slot_choice,
    gate_fixed,
    expert_gate,
    expert_up,
    expert_down,
    next_weights,
    hot_expert,
    slot_take,
):
    slot_count = lax.axis_size(("expert", "node", "inner"))
    tok_rows, model_width = tokens.shape
    pick_count = slot_choice.shape[1]
    capacity = max(2, 2 * tok_rows * pick_count // slot_count)
    flat_slot = slot_choice.reshape(-1)
    columns = jnp.arange(slot_count, dtype=jnp.int32)
    onehot = (flat_slot[:, None] == columns[None, :]).astype(jnp.int32)
    before = jnp.cumsum(onehot, axis=0) - onehot
    position = jnp.sum(before * onehot, axis=1)
    target = flat_slot * capacity + position
    source_rows = jnp.repeat(tokens, pick_count, axis=0)
    outgoing = (
        jnp.zeros((slot_count * capacity, model_width), jnp.bfloat16).at[target].set(source_rows)
    )
    outgoing = outgoing.reshape(slot_count, capacity, model_width)
    gate_matrix = expert_gate[0]
    up_matrix = expert_up[0]
    down_matrix = expert_down[0]
    block_rows = lax.all_to_all(
        outgoing, ("expert", "node", "inner"), split_axis=0, concat_axis=0, tiled=True
    )
    row_shape = block_rows.shape
    flat_rows = block_rows.reshape(-1, row_shape[-1])
    gate_value = jnp.dot(flat_rows, gate_matrix, preferred_element_type=jnp.float32)
    up_value = jnp.dot(flat_rows, up_matrix, preferred_element_type=jnp.float32)
    hidden = (jax.nn.silu(gate_value) * up_value).astype(jnp.bfloat16)
    result = jnp.dot(hidden, down_matrix, preferred_element_type=jnp.float32).astype(jnp.bfloat16)
    returned = lax.all_to_all(
        result.reshape(row_shape),
        ("expert", "node", "inner"),
        split_axis=0,
        concat_axis=0,
        tiled=True,
    )
    back_rows = returned.reshape(slot_count * capacity, model_width)[target]
    factors = gate_fixed.reshape(-1).astype(jnp.float32) * (1.0 / 65536.0)
    weighted = back_rows.astype(jnp.float32) * factors[:, None]
    moe_out = jnp.sum(weighted.reshape(tok_rows, pick_count, model_width), axis=1).astype(
        jnp.bfloat16
    )
    hot_count = hot_expert.shape[0]
    fetched = []
    for hot_index in range(hot_count):
        halves = spread(next_weights, ("expert", "node"), hot_expert[hot_index])
        fetched.append(lax.all_gather(halves, "inner", axis=2, tiled=True))
    take_index = slot_take[0]
    new_weights = jnp.zeros_like(fetched[0])
    for hot_index in range(hot_count):
        new_weights = jnp.where(take_index == hot_index, fetched[hot_index], new_weights)
    return (moe_out, new_weights)


def solution(mesh):
    return jax.shard_map(
        shards,
        mesh=mesh,
        in_specs=(
            P(("groups", "expert", "node", "inner"), None),
            P(("groups", "expert", "node", "inner"), None),
            P(("groups", "expert", "node", "inner"), None),
            P(("expert", "node"), None, None),
            P(("expert", "node"), None, None),
            P(("expert", "node"), None, None),
            P(("expert", "node"), None, "inner", None),
            P("groups"),
            P(("groups", "expert", "node", "inner")),
        ),
        out_specs=(
            P(("groups", "expert", "node", "inner"), None),
            P(("groups", "expert", "node", "inner"), None, None, None),
        ),
        check_vma=False,
    )
```

profile of v0, /device:TPU:11, one launch (start us, length us, event | category | flops | bytes accessed | tf_op | source)
XLA Modules:
  0.0 402.2 jit_solution(4920117343006732934)
XLA Ops:
  7.2 0.0 copy-start
  7.2 0.8 broadcast_multiply_fusion
  8.0 0.8 copy.13
  8.8 0.1 eq.47
  8.8 0.1 eq.43
  8.9 0.1 copy.12
  9.0 0.1 mul.51
  9.1 1.2 reduce-window.6
  10.3 0.2 slice_reduce_fusion
  10.5 0.1 fusion.16
  10.7 6.7 %scatter_custom_fusion = bf16[1024,2048]{1,0:T(8,128)(2,1)} fusion(s32[512]{0:T(512)S(1)} %bitcast.53, bf16[]{:T(256)} %constant.13.clone.1, bf16[64,2048]{1,0:T(8,128)(2,1)} %param.9), kind=kCustom, calls=%fused_computation.8 | custom fusion | bytes 4456450 | tf_op jit(solution)/shard_map/scatter | solution.py:35
  17.3 0.0 copy-start.2
  17.3 6.7 %all-to-all-start = ((bf16[16,64,2048]{2,1,0:T(8,128)(2,1)}), bf16[16,64,2048]{2,1,0:T(8,128)(2,1)}, u32[]{:S(2)}, u32[]{:S(2)}) async-start(bf16[16,64,2048]{2,1,0:T(8,128)(2,1)} %bitcast.51), calls=%async_computation | async-start | bytes 8388608 | tf_op jit(solution)/shard_map/all_to_all | solution.py:41
  24.0 0.0 all-reduce.3.cloned.1.call-start
  24.1 0.0 copy-done.2
  24.1 0.6 fusion.19
  26.0 4.2 %broadcast_select_fusion = (bf16[1,3,1024,384]{3,2,1,0:T(8,128)(2,1)}, bf16[1,3,1024,384]{3,2,1,0:T(8,128)(2,1)}) fusion(bf16[1,3,1024,384]{3,2,1,0:T(8,128)(2,1)} %param.15, pred[]{:T(512)S(6)} %eq.56, pred[]{:T(512)S(6)} %eq.53), kind=kLoop, calls=%fused_computation.6 | loop fusion | flops 2359296 | bytes 7077890 | tf_op jit(solution)/shard_map/jit(_where)/select_n | solution.py:8
  30.2 0.0 all-reduce.3.cloned.1.call-update
  30.2 0.0 copy-start.3
  30.2 0.0 all-gather.3.cloned.1.call-start
  30.2 237.4 %all-reduce.3.cloned.1.call-done = (bf16[1,3,1024,384]{3,2,1,0:T(8,128)(2,1)}, bf16[1,3,1024,384]{3,2,1,0:T(8,128)(2,1)}) async-done(((bf16[1,3,1024,384]{3,2,1,0:T(8,128)(2,1)}, bf16[1,3,1024,384]{3,2,1,0:T(8,128)(2,1)}), (bf16[1,3,1024,384]{3,2,1,0:T(8,128)(2,1)}, bf16[1,3,1024,384]{3,2,1,0:T(8,128)(2,1)})) %all-reduce.3.cloned.1.call-update) | async-done | bytes 4718608 | tf_op jit(solution)/shard_map/psum | solution.py:9
  267.6 0.0 all-gather.3.cloned.1.call-update
  267.6 0.0 all-to-all-done
  267.7 0.0 copy-done.3
  267.7 5.7 %fusion.7 = f32[1024,384]{1,0:T(8,128)} fusion(bf16[1024,2048]{1,0:T(8,128)(2,1)} %bitcast.5, bf16[1,2048,384]{2,1,0:T(8,128)(2,1)S(1)} %copy-done.3), kind=kOutput, calls=%fused_computation.14 | convolution fusion | flops 1610612736 | bytes 7340032 | tf_op jit(solution)/shard_map/dot_general | solution.py:46
  273.3 0.0 copy-done
  273.3 9.7 %convolution_convert_fusion = bf16[1024,2048]{1,0:T(8,128)(2,1)} fusion(bf16[1,384,2048]{2,1,0:T(8,128)(2,1)S(1)} %copy-done, f32[1024,384]{1,0:T(8,128)} %fusion.7, bf16[1024,2048]{1,0:T(8,128)(2,1)} %bitcast.5, bf16[1,2048,384]{2,1,0:T(8,128)(2,1)} %param.13), kind=kOutput, calls=%fused_computation.5 | convolution fusion | flops 3225681920 | bytes 13107200 | tf_op jit(solution)/shard_map/dot_general | solution.py:49
  283.0 8.0 %all-to-all-start.1 = ((bf16[16,64,2048]{2,1,0:T(8,128)(2,1)}), bf16[16,64,2048]{2,1,0:T(8,128)(2,1)}, u32[]{:S(2)}, u32[]{:S(2)}) async-start(bf16[16,64,2048]{2,1,0:T(8,128)(2,1)} %bitcast.52), calls=%async_computation.1 | async-start | bytes 8388608 | tf_op jit(solution)/shard_map/all_to_all | solution.py:50
  291.0 0.0 copy-start.1
  291.0 0.2 all-gather.5.cloned.1.call-start
  291.2 0.5 all-gather.5.cloned.1.call-update
  292.4 0.0 copy-done.1
  292.4 0.1 copy.16
  292.5 0.0 all-gather.3.cloned.1.call-done
  292.5 16.6 %all-gather.5.cloned.1.call-done = bf16[1,3,2048,384]{3,2,1,0:T(8,128)(2,1)} async-done(((bf16[1,3,1024,384]{3,2,1,0:T(8,128)(2,1)}), bf16[1,3,2048,384]{3,2,1,0:T(8,128)(2,1)}) %all-gather.5.cloned.1.call-update) | async-done | bytes 4718608 | tf_op jit(solution)/shard_map/all_gather | solution.py:67
  309.2 5.1 %select_select_fusion = bf16[1,3,2048,384]{3,2,1,0:T(8,128)(2,1)} fusion(bf16[1,3,2048,384]{3,2,1,0:T(8,128)(2,1)} %all-gather.3.cloned.1.call-done, bf16[1,3,2048,384]{3,2,1,0:T(8,128)(2,1)} %all-gather.5.cloned.1.call-done, pred[]{:T(512)} %bitcast.14, pred[]{:T(512)} %bitcast.12), kind=kLoop, calls=%fused_computation.2 | loop fusion | flops 4718592 | bytes 14155778 | tf_op jit(solution)/shard_map/jit(_where)/select_n | solution.py:71
  314.3 69.2 %all-to-all-done.1 = bf16[16,64,2048]{2,1,0:T(8,128)(2,1)} async-done(((bf16[16,64,2048]{2,1,0:T(8,128)(2,1)}), bf16[16,64,2048]{2,1,0:T(8,128)(2,1)}, u32[]{:S(2)}, u32[]{:S(2)}) %all-to-all-start.1) | async-done | bytes 4194336 | tf_op jit(solution)/shard_map/all_to_all | solution.py:50
  383.5 8.0 %gather_fusion = bf16[512,2048]{1,0:T(8,128)(2,1)} fusion(bf16[1024,2048]{1,0:T(8,128)(2,1)} %bitcast.10, s32[1024]{0:T(1024)S(1)} %pad_clamp_fusion), kind=kCustom, calls=%fused_computation | custom fusion | bytes 4196352 | tf_op jit(solution)/shard_map/gather | solution.py:57
  391.5 4.1 %fusion = bf16[64,2048]{1,0:T(8,128)(2,1)} fusion(bf16[512,2048]{1,0:T(8,128)(2,1)} %gather_fusion, f32[64,8]{1,0:T(8,128)S(1)} %copy.16), kind=kLoop, calls=%fused_computation.4 | loop fusion | flops 3014656 | bytes 2361344 | tf_op jit(solution)/shard_map/reduce_sum | solution.py:60
  (6 shorter events, 0.1 us)
Async XLA Ops:
  7.2 266.2 %copy-start = (bf16[1,384,2048]{2,1,0:T(8,128)(2,1)S(1)}, bf16[1,384,2048]{2,1,0:T(8,128)(2,1)}, u32[]{:S(2)}) copy-start(bf16[1,384,2048]{2,1,0:T(8,128)(2,1)} %param.14) | copy-start | bytes 4718596
  17.3 6.7 %copy-start.2 = (s32[2]{0:T(128)S(1)}, s32[2]{0:T(128)}, u32[]{:S(2)}) copy-start(s32[2]{0:T(128)} %param.16) | copy-start | bytes 28
  17.3 250.3 %all-to-all-start = ((bf16[16,64,2048]{2,1,0:T(8,128)(2,1)}), bf16[16,64,2048]{2,1,0:T(8,128)(2,1)}, u32[]{:S(2)}, u32[]{:S(2)}) async-start(bf16[16,64,2048]{2,1,0:T(8,128)(2,1)} %bitcast.51), calls=%async_computation | async-start | bytes 8388608 | tf_op jit(solution)/shard_map/all_to_all | solution.py:41
  24.0 243.6 %all-reduce.3.cloned.1.call-start = ((), (), s32[]{:S(2)}) async-start(), calls=%async_computation.4 | async-start | bytes 9437184 | tf_op jit(solution)/shard_map/psum | solution.py:9
  30.2 237.5 %copy-start.3 = (bf16[1,2048,384]{2,1,0:T(8,128)(2,1)S(1)}, bf16[1,2048,384]{2,1,0:T(8,128)(2,1)}, u32[]{:S(2)}) copy-start(bf16[1,2048,384]{2,1,0:T(8,128)(2,1)} %param.12) | copy-start | bytes 4718596
  30.2 262.4 %all-gather.3.cloned.1.call-start = ((), (), s32[]{:S(2)}) async-start(), calls=%async_computation.2 | async-start | bytes 7077888 | tf_op jit(solution)/shard_map/all_gather | solution.py:67
  283.0 100.4 %all-to-all-start.1 = ((bf16[16,64,2048]{2,1,0:T(8,128)(2,1)}), bf16[16,64,2048]{2,1,0:T(8,128)(2,1)}, u32[]{:S(2)}, u32[]{:S(2)}) async-start(bf16[16,64,2048]{2,1,0:T(8,128)(2,1)} %bitcast.52), calls=%async_computation.1 | async-start | bytes 8388608 | tf_op jit(solution)/shard_map/all_to_all | solution.py:50
  291.0 1.4 copy-start.1
  291.0 18.2 %all-gather.5.cloned.1.call-start = ((), (), s32[]{:S(2)}) async-start(), calls=%async_computation.3 | async-start | bytes 7077888 | tf_op jit(solution)/shard_map/all_gather | solution.py:67
Sparse Core Ops, SparseCore 0:
  30.3 237.2 all-reduce.2
  269.2 16.0 all-gather.2
  293.4 15.7 all-gather.4
where the time goes:
time: 403 us; the launch traced here: 402 us
  waiting for transfers between devices  324 us (80%)
  local copies, waits for them, and re-layouts  16.7 us (4%)
  between operations  15.8 us (4%)
  other arithmetic  15.6 us (4%)
  matrix products  15.4 us (4%)
  starting transfers between devices  15 us (4%)
    psum x1, waiting for transfers between devices, spread(): return lax.psum(block, axis)  237 us
    all_to_all x1, waiting for transfers between devices, shards(): lax.all_to_all(result.reshape(row_shape), ('expert', 'node', 'inner'), sp...  69.2 us
    all_gather x2, waiting for transfers between devices, shards(): fetched.append(lax.all_gather(halves, 'inner', axis=2, tiled=True))  16.7 us
    dot_general x1, matrix products, shards(): jnp.dot(hidden, down_matrix, preferred_element_type=jnp.float32)  9.71 us
  transfers between devices with their start and end apart: 5, of which 3 were waited for; matrix products, arithmetic and copies ran while one was open for 6% of the time, Pallas kernels for 0%

commit v1 on v0

v1 whole, which is shorter than its diff:
```python
import functools

import jax
import jax.numpy as jnp
from jax import lax
from jax.experimental import pallas as pl
from jax.experimental.pallas import tpu as pltpu
from jax.sharding import PartitionSpec as P

MESH = pl.DeviceIdType.MESH
BF16 = jnp.bfloat16
F32 = jnp.float32
KINDS = 3


def routed(tokens, slot_choice, gate_fixed, expert_gate, expert_up, expert_down):
    slot_count = lax.axis_size(("expert", "node", "inner"))
    tok_rows, model_width = tokens.shape
    pick_count = slot_choice.shape[1]
    capacity = max(2, 2 * tok_rows * pick_count // slot_count)
    flat_slot = slot_choice.reshape(-1)
    columns = jnp.arange(slot_count, dtype=jnp.int32)
    onehot = (flat_slot[:, None] == columns[None, :]).astype(jnp.int32)
    before = jnp.cumsum(onehot, axis=0) - onehot
    position = jnp.sum(before * onehot, axis=1)
    target = flat_slot * capacity + position
    source_rows = jnp.repeat(tokens, pick_count, axis=0)
    outgoing = jnp.zeros((slot_count * capacity, model_width), BF16).at[target].set(source_rows)
    outgoing = outgoing.reshape(slot_count, capacity, model_width)
    axes = ("expert", "node", "inner")
    block_rows = lax.all_to_all(outgoing, axes, split_axis=0, concat_axis=0, tiled=True)
    flat_rows = block_rows.reshape(-1, model_width)
    gate_value = jnp.dot(flat_rows, expert_gate[0], preferred_element_type=F32)
    up_value = jnp.dot(flat_rows, expert_up[0], preferred_element_type=F32)
    hidden = (jax.nn.silu(gate_value) * up_value).astype(BF16)
    result = jnp.dot(hidden, expert_down[0], preferred_element_type=F32).astype(BF16)
    returned = lax.all_to_all(
        result.reshape(block_rows.shape), axes, split_axis=0, concat_axis=0, tiled=True
    )
    back_rows = returned.reshape(slot_count * capacity, model_width)[target]
    factors = gate_fixed.reshape(-1).astype(F32) * (1.0 / 65536.0)
    weighted = back_rows.astype(F32) * factors[:, None]
    return jnp.sum(weighted.reshape(tok_rows, pick_count, model_width), axis=1).astype(BF16)


def pick(condition, yes, no):
    return lax.select_n(condition, no, yes)


def kernel(sizes, dense, *refs):
    ng, nz, nx, ni = sizes
    refs = list(refs)
    nw, hot, take = refs[:3]
    del refs[:3]
    if dense:
        tokens, factors, w_gate, w_up, w_down = refs[:5]
        del refs[:5]
        moe_out = refs.pop(0)
    out = refs.pop(0)
    (meta, meta_y, meta_i, xin, up, dn, full, own_out, peer_out) = refs[:9]
    del refs[:9]
    (m_send, m_recv, s1s, s1r, ups, upr, dns, dnr, xs, xr, ys, yr, os, ps, pr) = refs[:15]
    del refs[:15]

    g, z, x, i = (lax.axis_index(a) for a in ("groups", "expert", "node", "inner"))
    half = nw.shape[2]
    part = half // (nx * ng)
    experts = nz * nx
    unions = 1 + ng
    items = KINDS * unions
    above, below = lax.rem(z + 1, nz), lax.rem(z + nz - 1, nz)

    def rows(p, q):
        return pl.ds(pl.multiple_of((p * ng + q) * part, part), part)

    def remote(src, dst, send, recv, **where):
        return pltpu.make_async_remote_copy(
            src_ref=src, dst_ref=dst, send_sem=send, recv_sem=recv, device_id=where, device_id_type=MESH
        )

    barrier = pltpu.get_barrier_semaphore()

    def greet(**where):
        pl.semaphore_signal(barrier, inc=1, device_id=where, device_id_type=MESH)

    for d in range(1, nx):
        greet(node=lax.rem(x + d, nx))
    for d in range(1, ng):
        greet(groups=lax.rem(g + d, ng))
    for d in range(1, ni):
        greet(inner=lax.rem(i + d, ni))

    @pl.when(z > 0)
    def _():
        greet(expert=below)

    @pl.when(z < nz - 1)
    def _():
        greet(expert=above)

    ends = (z > 0).astype(jnp.int32) + (z < nz - 1).astype(jnp.int32)
    pl.semaphore_wait(barrier, nx - 1 + ng - 1 + ni - 1 + ends)

    last = experts - 1
    other = hot[0] + hot[1] - last
    last_place = pick(hot[0] == last, jnp.int32(0), jnp.int32(1))
    code = pick(take[0] == 2, jnp.int32(2), pick(take[0] == last_place, jnp.int32(0), jnp.int32(1)))
    line = lax.broadcasted_iota(jnp.int32, meta.shape, 0)
    meta[...] = jnp.where(line == 0, other, code)
    meta_copies = []
    for d in range(1, ng):
        n = len(meta_copies)
        meta_copies.append(
            remote(meta, meta_y.at[d - 1], m_send.at[n], m_recv.at[n], groups=lax.rem(g + d, ng))
        )
    for d in range(1, ni):
        n = len(meta_copies)
        meta_copies.append(
            remote(meta, meta_i.at[d - 1], m_send.at[n], m_recv.at[n], inner=lax.rem(i + d, ni))
        )
    for copy in meta_copies:
        copy.start()

    if dense:
        (tok, fac, acc, res, xres, rup, rdn) = refs[:7]
        (tus, tur, tds, tdr, txs, txr, fus, fur, fds, fdr, fxs, fxr, rxs, rxr, rus, rur, rds, rdr) = refs[7:]
        tok_rows = tokens.shape[0]

        def tok_up(b):
            return [
                remote(tok.at[x, b], tok.at[x, b], tus.at[b], tur.at[b], expert=above),
                remote(fac.at[x, b], fac.at[x, b], fus.at[b], fur.at[b], expert=above),
            ]

        def tok_dn(b):
            return [
                remote(tok.at[x, b], tok.at[x, b], tds.at[b], tdr.at[b], expert=below),
                remote(fac.at[x, b], fac.at[x, b], fds.at[b], fdr.at[b], expert=below),
            ]

        def tok_x(d, b, col):
            to = lax.rem(x + d, nx)
            return [
                remote(tok.at[col, b], tok.at[col, b], txs.at[d - 1, b], txr.at[d - 1, b], node=to),
                remote(fac.at[col, b], fac.at[col, b], fxs.at[d - 1, b], fxr.at[d - 1, b], node=to),
            ]

        tok[x, z] = tokens[...]
        fac[x, z] = factors[...]

        def tok_step(s, carry):
            bu, bd = z - s, z + s

            @pl.when(bu >= 0)
            def _():
                @pl.when(s > 0)
                def _():
                    for c in tok_up(bu):
                        c.wait_recv()

                @pl.when(z < nz - 1)
                def _():
                    for c in tok_up(bu):
                        c.start()

                for d in range(1, nx):
                    for c in tok_x(d, bu, x):
                        c.start()

            @pl.when(bd < nz)
            def _():
                @pl.when(s > 0)
                def _():
                    for c in tok_dn(bd):
                        c.wait_recv()

                @pl.when(z > 0)
                def _():
                    for c in tok_dn(bd):
                        c.start()

                @pl.when(s > 0)
                def _():
                    for d in range(1, nx):
                        for c in tok_x(d, bd, x):
                            c.start()

            return carry

    def first(d, k):
        to = lax.rem(x + d, nx)
        return remote(nw.at[0, k, rows(to, g)], xin.at[d - 1, k], s1s.at[d - 1, k], s1r.at[d - 1, k], node=to)

    def start_first():
        for k in range(KINDS):
            for d in range(1, nx):
                first(d, k).start()

    def up_copy(j):
        return remote(up.at[j], up.at[j], ups.at[j], upr.at[j], expert=above)

    def dn_copy(j):
        return remote(dn.at[j], dn.at[j], dns.at[j], dnr.at[j], expert=below)

    def x_copy(d, j, p):
        k, u = j // unions, j % unions
        spot = full.at[u, k, p, g]
        return remote(spot, spot, xs.at[d - 1, j], xr.at[d - 1, j], node=lax.rem(x + d, nx))

    def y_copy(d, j, p, q):
        k, u = j // unions, j % unions
        spot = full.at[u, k, p, q]
        return remote(spot, spot, ys.at[d - 1, j, p], yr.at[d - 1, j, p], groups=lax.rem(g + d, ng))

    def y_wanted(d, j):
        u = j % unions
        return (u == 0) | (u == 1 + lax.rem(g + d, ng))

    def y_start(j, p):
        for d in range(1, ng):
            @pl.when(y_wanted(d, j))
            def _():
                y_copy(d, j, p, g).start()

    def hot_loop():
        others = [other] + [jnp.max(meta_y[d - 1, 0:1, :]) for d in range(1, ng)]

        def owner(u):
            expert = jnp.int32(last)
            for d in range(ng):
                expert = pick(u == 1 + lax.rem(g + ng - d, ng), others[d], expert)
            return expert // nx, expert % nx

        def here(j):
            k, u = j // unions, j % unions
            oz, ox = owner(u)
            value = nw[0, k, rows(x, g), :]
            for d in range(1, nx):
                value = pick(ox == lax.rem(x + nx - d, nx), xin[d - 1, k], value)
            return oz, value

        def line_step(j, buffer, copy, first_one, last_one):
            @pl.when((j >= 0) & (j < items))
            def _():
                oz, value = here(j)

                @pl.when(first_one)
                def _():
                    buffer[j] = value

                @pl.when(jnp.logical_not(first_one))
                def _():
                    copy(j).wait_recv()
                    buffer[j] = pick(oz == z, value, buffer[j])

                @pl.when(jnp.logical_not(last_one))
                def _():
                    copy(j).start()

        lag = 2
        far = jnp.maximum(z, nz - 1 - z)

        def step(s, carry):
            line_step(s - z, up, up_copy, z == 0, z == nz - 1)
            line_step(s - (nz - 1 - z), dn, dn_copy, z == nz - 1, z == 0)
            j = s - far

            @pl.when((j >= 0) & (j < items))
            def _():
                k, u = j // unions, j % unions
                oz, _ = owner(u)
                full[u, k, x, g] = pick(oz <= z, up[j], dn[j])
                for d in range(1, nx):
                    x_copy(d, j, x).start()
                y_start(j, x)

            j2 = j - lag

            @pl.when((j2 >= 0) & (j2 < items))
            def _():
                for d in range(1, nx):
                    p = lax.rem(x + nx - d, nx)
                    x_copy(d, j2, p).wait_recv()
                    y_start(j2, p)

            return carry

        lax.fori_loop(0, items + nz - 1 + lag, step, 0)

    def out_rows():
        return pl.ds(pl.multiple_of(i * half, half), half)

    def own_copy(k):
        return pltpu.make_async_copy(own_out.at[k], out.at[0, k, out_rows()], os.at[k])

    def peer_copy(d, k):
        to = lax.rem(i + d, ni)
        return remote(peer_out.at[d - 1, k], out.at[0, k, out_rows()], ps.at[d - 1, k], pr.at[d - 1, k], inner=to)

    def finish_hot():
        codes = [jnp.max(meta_i[d - 1, 1:2, :]) for d in range(1, ni)]
        for k in range(KINDS):
            for d in range(1, ng):
                q = lax.rem(g + ng - d, ng)
                for p in range(nx):
                    y_copy(d, k * unions, p, q).wait_recv()
                    y_copy(d, k * unions + 1 + g, p, q).wait_recv()
            known = full[0, k].reshape(half, full.shape[-1])
            second = full[1 + g, k].reshape(half, full.shape[-1])

            def chosen(c):
                return pick(c == 2, jnp.zeros_like(known), pick(c == 0, known, second))

            for d in range(1, ni):
                peer_out[d - 1, k] = chosen(codes[ni - d - 1])
                peer_copy(d, k).start()
            own_out[k] = chosen(code)
            own_copy(k).start()

    def drain():
        for copy in meta_copies:
            copy.wait_send()
        for k in range(KINDS):
            for d in range(1, nx):
                first(d, k).wait_send()

        def sends(j, carry):
            @pl.when(z < nz - 1)
            def _():
                up_copy(j).wait_send()

            @pl.when(z > 0)
            def _():
                dn_copy(j).wait_send()

            for d in range(1, nx):
                x_copy(d, j, x).wait_send()
            for d in range(1, ng):
                @pl.when(y_wanted(d, j))
                def _():
                    for p in range(nx):
                        y_copy(d, j, p, g).wait_send()
            return carry

        lax.fori_loop(0, items, sends, 0)
        for k in range(KINDS):
            own_copy(k).wait()
            for d in range(1, ni):
                peer_copy(d, k).wait_send()
                peer_copy(d, k).wait_recv()

    if dense:
        def apply(col):
            count = nz * tok_rows
            block = tok[col].reshape(count, tok.shape[-1])
            gate_value = jnp.dot(block, w_gate[0], preferred_element_type=F32)
            up_value = jnp.dot(block, w_up[0], preferred_element_type=F32)
            hidden = gate_value / (1.0 + jnp.exp(-gate_value)) * up_value
            row = lax.broadcasted_iota(jnp.int32, (tok_rows, fac.shape[-1]), 0)
            column = lax.broadcasted_iota(jnp.int32, (tok_rows, fac.shape[-1]), 1)
            weights = []
            for b in range(nz):
                line_of = fac[col, b, pl.ds(z * nx + x, 1), :]
                weights.append(jnp.sum(jnp.where(row == column, line_of, 0.0), axis=1, keepdims=True))
            hidden = (hidden * jnp.concatenate(weights, axis=0)).astype(BF16)
            return jnp.dot(hidden, w_down[0], preferred_element_type=F32).reshape(nz, tok_rows, -1)

        def res_copy(d):
            return remote(res.at[d - 1], xres.at[d - 1], rxs.at[d - 1], rxr.at[d - 1], node=lax.rem(x + nx - d, nx))

        def rup_copy(b):
            return remote(rup.at[b], rup.at[b], rus.at[b], rur.at[b], expert=above)

        def rdn_copy(b):
            return remote(rdn.at[b], rdn.at[b], rds.at[b], rdr.at[b], expert=below)

        def sum_step(s, carry):
            iu, id_ = s - z, s - (nz - 1 - z)
            bu, bd = nz - 1 - iu, id_

            @pl.when((iu >= 0) & (bu > z))
            def _():
                @pl.when(z == 0)
                def _():
                    rup[bu] = acc[bu].astype(BF16)

                @pl.when(z > 0)
                def _():
                    rup_copy(bu).wait_recv()
                    rup[bu] = (acc[bu] + rup[bu].astype(F32)).astype(BF16)

                rup_copy(bu).start()

            @pl.when((id_ >= 0) & (bd < z))
            def _():
                @pl.when(z == nz - 1)
                def _():
                    rdn[bd] = acc[bd].astype(BF16)

                @pl.when(z < nz - 1)
                def _():
                    rdn_copy(bd).wait_recv()
                    rdn[bd] = (acc[bd] + rdn[bd].astype(F32)).astype(BF16)

                rdn_copy(bd).start()

            return carry

        def finish_sum():
            @pl.when(z > 0)
            def _():
                rup_copy(z).wait_recv()
                acc[z] = acc[z] + rup[z].astype(F32)

            @pl.when(z < nz - 1)
            def _():
                rdn_copy(z).wait_recv()
                acc[z] = acc[z] + rdn[z].astype(F32)

            moe_out[...] = acc[z].astype(BF16)

        def drain_moe():
            def sends(b, carry):
                @pl.when((b <= z) & (z < nz - 1))
                def _():
                    for c in tok_up(b):
                        c.wait_send()

                @pl.when((b >= z) & (z > 0))
                def _():
                    for c in tok_dn(b):
                        c.wait_send()

                for d in range(1, nx):
                    for c in tok_x(d, b, x):
                        c.wait_send()

                @pl.when(b > z)
                def _():
                    rup_copy(b).wait_send()

                @pl.when(b < z)
                def _():
                    rdn_copy(b).wait_send()

                return carry

            lax.fori_loop(0, nz, sends, 0)
            for d in range(1, nx):
                res_copy(d).wait_send()

        lax.fori_loop(0, 1, tok_step, 0)
        start_first()
        lax.fori_loop(1, nz, tok_step, 0)
        acc[...] = apply(x)
        for d in range(1, nx):
            col = lax.rem(x + nx - d, nx)
            for b in range(nz):
                for c in tok_x(d, b, col):
                    c.wait_recv()
            res[d - 1] = apply(col).astype(BF16)
            res_copy(d).start()
    else:
        start_first()

    for copy in meta_copies:
        copy.wait_recv()
    for k in range(KINDS):
        for d in range(1, nx):
            first(d, k).wait_recv()
    hot_loop()
    if dense:
        for d in range(1, nx):
            res_copy(d).wait_recv()
            acc[...] = acc[...] + xres[d - 1].astype(F32)
        lax.fori_loop(0, 2 * nz - 2, sum_step, 0)
        finish_sum()
        drain_moe()
    finish_hot()
    drain()


def shards(
    tokens,
    slot_choice,
    gate_fixed,
    expert_gate,
    expert_up,
    expert_down,
    next_weights,
    hot_expert,
    slot_take,
):
    sizes = tuple(lax.axis_size(a) for a in ("groups", "expert", "node", "inner"))
    ng, nz, nx, ni = sizes
    tok_rows, width = tokens.shape
    _, kinds, half, hidden = next_weights.shape
    assert kinds == KINDS and hot_expert.shape[0] == 2
    experts = nz * nx
    dense = experts * ni <= 2 * slot_choice.shape[1]
    part = half // (nx * ng)
    items = KINDS * (1 + ng)
    vmem, smem = (pl.BlockSpec(memory_space=s) for s in (pltpu.VMEM, pltpu.SMEM))
    dma = pltpu.SemaphoreType.DMA
    operands, specs = [next_weights, hot_expert, slot_take], [vmem, smem, smem]
    outs = [jax.ShapeDtypeStruct((1, KINDS, ni * half, hidden), BF16)]
    out_specs = [pl.BlockSpec(memory_space=pl.ANY)]
    dx, dg, di = max(nx - 1, 1), max(ng - 1, 1), max(ni - 1, 1)
    scratch = [
        pltpu.VMEM((8, 128), jnp.int32),
        pltpu.VMEM((dg, 8, 128), jnp.int32),
        pltpu.VMEM((di, 8, 128), jnp.int32),
        pltpu.VMEM((dx, KINDS, part, hidden), BF16),
        pltpu.VMEM((items, part, hidden), BF16),
        pltpu.VMEM((items, part, hidden), BF16),
        pltpu.VMEM((1 + ng, KINDS, nx, ng, part, hidden), BF16),
        pltpu.VMEM((KINDS, half, hidden), BF16),
        pltpu.VMEM((di, KINDS, half, hidden), BF16),
        dma((dg + di,)), dma((dg + di,)),
        dma((dx, KINDS)), dma((dx, KINDS)),
        dma((items,)), dma((items,)),
        dma((items,)), dma((items,)),
        dma((dx, items)), dma((dx, items)),
        dma((dg, items, nx)), dma((dg, items, nx)),
        dma((KINDS,)),
        dma((di, KINDS)), dma((di, KINDS)),
    ]
    if dense:
        owner = slot_choice // ni
        share = gate_fixed.astype(F32) * (1.0 / 65536.0)
        tall, wide = -(-experts // 8) * 8, -(-tok_rows // 128) * 128
        named = owner[None] == jnp.arange(tall, dtype=jnp.int32)[:, None, None]
        factors = jnp.sum(jnp.where(named, share[None], 0.0), axis=2)
        factors = jnp.pad(factors, ((0, 0), (0, wide - tok_rows)))
        operands += [tokens, factors, expert_gate, expert_up, expert_down]
        specs += [vmem] * 5
        outs = [jax.ShapeDtypeStruct((tok_rows, width), BF16)] + outs
        out_specs = [vmem] + out_specs
        scratch += [
            pltpu.VMEM((nx, nz, tok_rows, width), BF16),
            pltpu.VMEM((nx, nz, tall, wide), F32),
            pltpu.VMEM((nz, tok_rows, width), F32),
            pltpu.VMEM((dx, nz, tok_rows, width), BF16),
            pltpu.VMEM((dx, nz, tok_rows, width), BF16),
            pltpu.VMEM((nz, tok_rows, width), BF16),
            pltpu.VMEM((nz, tok_rows, width), BF16),
            dma((nz,)), dma((nz,)), dma((nz,)), dma((nz,)), dma((dx, nz)), dma((dx, nz)),
            dma((nz,)), dma((nz,)), dma((nz,)), dma((nz,)), dma((dx, nz)), dma((dx, nz)),
            dma((dx,)), dma((dx,)),
            dma((nz,)), dma((nz,)), dma((nz,)), dma((nz,)),
        ]
    results = pl.pallas_call(
        functools.partial(kernel, sizes, dense),
        out_shape=outs,
        in_specs=specs,
        out_specs=out_specs,
        scratch_shapes=scratch,
        compiler_params=pltpu.CompilerParams(
            collective_id=0, has_side_effects=True, vmem_limit_bytes=56 * 2**20
        ),
    )(*operands)
    if dense:
        return tuple(results)
    moe_out = routed(tokens, slot_choice, gate_fixed, expert_gate, expert_up, expert_down)
    return moe_out, results[0]


def solution(mesh):
    tokens_spec = P(("groups", "expert", "node", "inner"), None)
    weights_spec = P(("expert", "node"), None, None)
    return jax.shard_map(
        shards,
        mesh=mesh,
        in_specs=(
            tokens_spec,
            tokens_spec,
            tokens_spec,
            weights_spec,
            weights_spec,
            weights_spec,
            P(("expert", "node"), None, "inner", None),
            P("groups"),
            P(("groups", "expert", "node", "inner")),
        ),
        out_specs=(tokens_spec, P(("groups", "expert", "node", "inner"), None, None, None)),
        check_vma=False,
    )
```

time: 403 us -> 147 us (0.36)
  the two profiles are of different devices: /device:TPU:11 before, /device:TPU:0 now
where the time goes in v1:
time: 147 us
  Pallas kernels  137 us (93%)
  local copies, waits for them, and re-layouts  7.26 us (5%)
    pallas_call x1, Pallas kernels, shards(): pl.pallas_call(functools.partial(kernel, sizes, dense), out_shape=outs, i...  137 us
    unnamed x2, local copies, waits for them, and re-layouts  6.66 us

profile of v1, /device:TPU:0, one launch (start us, length us, event | category | flops | bytes accessed | tf_op | source)
XLA Modules:
  0.0 147.1 jit_solution(13048122789097973324)
XLA Ops:
  1.3 0.7 add_select_fusion
  2.0 0.7 convert_multiply_fusion
  2.7 0.6 pad.4.refs_4_
  3.3 137.2 %shard_map.104 = (bf16[64,2048]{1,0:T(8,128)(2,1)}, bf16[1,3,2048,384]{3,2,1,0:T(8,128)(2,1)}) custom-call(bf16[1,3,1024,384]{3,2,1,0:T(8,128)(2,1)} %refs_0_.1, s32[2]{0:T(128)} %refs_1_.1, s32[1]{0:T(128)S(6)} %copy.15.refs_2_, bf16[64,2048]{1,0:T(8,128)(2,1)} %refs_3_.1, f32[8,128]{1,0:T(8,128)} %pad.4.refs_4_, bf16[1,2048,384]{2,1,0:T(8,128)(2,1)} %refs_5_.1, ...), custom_call_target="tpu_custom_call" | custom-call | tf_op jit(solution)/shard_map/pallas_call | solution.py:552
  140.5 1.7 %copy.16 = bf16[64,2048]{1,0:T(8,128)(2,1)} copy(bf16[64,2048]{1,0:T(8,128)(2,1)} %get-tuple-element.4) | data formatting | bytes 524288
  142.1 5.0 %copy.17 = bf16[1,3,2048,384]{3,2,1,0:T(8,128)(2,1)} copy(bf16[1,3,2048,384]{3,2,1,0:T(8,128)(2,1)} %get-tuple-element.5) | data formatting | bytes 9437184
  (1 shorter events, 0.0 us)

commit v2 on v1

--- a/solution.py
+++ b/solution.py
@@ -53,7 +53,7 @@
     nw, hot, take = refs[:3]
     del refs[:3]
     if dense:
-        tokens, factors, w_gate, w_up, w_down = refs[:5]
+        tokens, factors, *w_in = refs[:5]
         del refs[:5]
         moe_out = refs.pop(0)
     out = refs.pop(0)
@@ -122,6 +122,14 @@
         copy.start()
 
     if dense:
+        (w_gate, w_up, w_down, w_sem) = refs[:4]
+        del refs[:4]
+        load_copies = [
+            pltpu.make_async_copy(src, dst, w_sem.at[n])
+            for n, (src, dst) in enumerate(zip(w_in, (w_gate, w_up, w_down)))
+        ]
+        for copy in load_copies:
+            copy.start()
         (tok, fac, acc, res, xres, rup, rdn) = refs[:7]
         (tus, tur, tds, tdr, txs, txr, fus, fur, fds, fdr, fxs, fxr, rxs, rxr, rus, rur, rds, rdr) = refs[7:]
         tok_rows = tokens.shape[0]
@@ -222,7 +230,7 @@
             def _():
                 y_copy(d, j, p, g).start()
 
-    def hot_loop():
+    def hot_steps():
         others = [other] + [jnp.max(meta_y[d - 1, 0:1, :]) for d in range(1, ng)]
 
         def owner(u):
@@ -258,9 +266,16 @@
                     copy(j).start()
 
         lag = 2
-        far = jnp.maximum(z, nz - 1 - z)
+        far, near = jnp.maximum(z, nz - 1 - z), jnp.minimum(z, nz - 1 - z)
 
         def step(s, carry):
+            j1 = s - near
+
+            @pl.when((j1 >= 0) & (j1 < items) & (j1 % unions == 0))
+            def _():
+                for d in range(1, nx):
+                    first(d, j1 // unions).wait_recv()
+
             line_step(s - z, up, up_copy, z == 0, z == nz - 1)
             line_step(s - (nz - 1 - z), dn, dn_copy, z == nz - 1, z == 0)
             j = s - far
@@ -285,7 +300,7 @@
 
             return carry
 
-        lax.fori_loop(0, items + nz - 1 + lag, step, 0)
+        return step, items + nz - 1 + lag
 
     def out_rows():
         return pl.ds(pl.multiple_of(i * half, half), half)
@@ -449,10 +464,20 @@
             for d in range(1, nx):
                 res_copy(d).wait_send()
 
-        lax.fori_loop(0, 1, tok_step, 0)
         start_first()
-        lax.fori_loop(1, nz, tok_step, 0)
+        lax.fori_loop(0, nz, tok_step, 0)
+    else:
+        start_first()
+    for copy in meta_copies:
+        copy.wait_recv()
+    hot_step, hot_count = hot_steps()
+    if dense:
+        at_own, at_other, at_sum = (hot_count * n // 14 for n in (2, 5, 10))
+        lax.fori_loop(0, at_own, hot_step, 0)
+        for copy in load_copies:
+            copy.wait()
         acc[...] = apply(x)
+        lax.fori_loop(at_own, at_other, hot_step, 0)
         for d in range(1, nx):
             col = lax.rem(x + nx - d, nx)
             for b in range(nz):
@@ -460,23 +485,23 @@
                     c.wait_recv()
             res[d - 1] = apply(col).astype(BF16)
             res_copy(d).start()
-    else:
-        start_first()
-
-    for copy in meta_copies:
-        copy.wait_recv()
-    for k in range(KINDS):
-        for d in range(1, nx):
-            first(d, k).wait_recv()
-    hot_loop()
-    if dense:
+        lax.fori_loop(at_other, at_sum, hot_step, 0)
         for d in range(1, nx):
             res_copy(d).wait_recv()
             acc[...] = acc[...] + xres[d - 1].astype(F32)
-        lax.fori_loop(0, 2 * nz - 2, sum_step, 0)
+
+        def both(s, carry):
+            hot_step(s, carry)
+            return sum_step(s - at_sum, carry)
+
+        lax.fori_loop(at_sum, hot_count, both, 0)
+        lax.fori_loop(hot_count - at_sum, 2 * nz - 2, sum_step, 0)
+        finish_hot()
         finish_sum()
         drain_moe()
-    finish_hot()
+    else:
+        lax.fori_loop(0, hot_count, hot_step, 0)
+        finish_hot()
     drain()
 
 
@@ -533,10 +558,14 @@
         factors = jnp.sum(jnp.where(named, share[None], 0.0), axis=2)
         factors = jnp.pad(factors, ((0, 0), (0, wide - tok_rows)))
         operands += [tokens, factors, expert_gate, expert_up, expert_down]
-        specs += [vmem] * 5
+        specs += [vmem] * 2 + [pl.BlockSpec(memory_space=pl.ANY)] * 3
         outs = [jax.ShapeDtypeStruct((tok_rows, width), BF16)] + outs
         out_specs = [vmem] + out_specs
         scratch += [
+            pltpu.VMEM(expert_gate.shape, BF16),
+            pltpu.VMEM(expert_up.shape, BF16),
+            pltpu.VMEM(expert_down.shape, BF16),
+            dma((3,)),
             pltpu.VMEM((nx, nz, tok_rows, width), BF16),
             pltpu.VMEM((nx, nz, tall, wide), F32),
             pltpu.VMEM((nz, tok_rows, width), F32),

time: 147 us -> 129 us (0.88)
  Pallas kernels: 137 us -> 119 us
    pallas_call x1, Pallas kernels: 137 us -> 119 us  [shards(): pl.pallas_call(functools.partial(kernel, sizes, dense), out_shape=outs, i...]
where the time goes in v2:
time: 129 us
  Pallas kernels  119 us (92%)
  local copies, waits for them, and re-layouts  7.26 us (6%)
  other arithmetic  1.4 us (1%)
  between operations  1.29 us (1%)
    pallas_call x1, Pallas kernels, shards(): pl.pallas_call(functools.partial(kernel, sizes, dense), out_shape=outs, i...  119 us
    unnamed x2, local copies, waits for them, and re-layouts  6.66 us

profile of v2, /device:TPU:0, one launch (start us, length us, event | category | flops | bytes accessed | tf_op | source)
XLA Modules:
  0.0 128.9 jit_solution(7915175970178790627)
XLA Ops:
  1.3 0.7 add_select_fusion
  2.0 0.7 convert_multiply_fusion
  2.7 0.6 pad.4.refs_4_
  3.3 119.0 %shard_map.104 = (bf16[64,2048]{1,0:T(8,128)(2,1)}, bf16[1,3,2048,384]{3,2,1,0:T(8,128)(2,1)}) custom-call(bf16[1,3,1024,384]{3,2,1,0:T(8,128)(2,1)} %refs_0_.1, s32[2]{0:T(128)} %refs_1_.1, s32[1]{0:T(128)S(6)} %copy.15.refs_2_, bf16[64,2048]{1,0:T(8,128)(2,1)} %refs_3_.1, f32[8,128]{1,0:T(8,128)} %pad.4.refs_4_, bf16[1,2048,384]{2,1,0:T(8,128)(2,1)} %refs_5_.1, ...), custom_call_target="tpu_custom_call" | custom-call | tf_op jit(solution)/shard_map/pallas_call | solution.py:581
  122.3 1.7 %copy.16 = bf16[64,2048]{1,0:T(8,128)(2,1)} copy(bf16[64,2048]{1,0:T(8,128)(2,1)} %get-tuple-element.4) | data formatting | bytes 524288
  123.9 5.0 %copy.17 = bf16[1,3,2048,384]{3,2,1,0:T(8,128)(2,1)} copy(bf16[1,3,2048,384]{3,2,1,0:T(8,128)(2,1)} %get-tuple-element.5) | data formatting | bytes 9437184
  (1 shorter events, 0.0 us)

commit v3 on v2

--- a/solution.py
+++ b/solution.py
@@ -134,63 +134,64 @@
         (tus, tur, tds, tdr, txs, txr, fus, fur, fds, fdr, fxs, fxr, rxs, rxr, rus, rur, rds, rdr) = refs[7:]
         tok_rows = tokens.shape[0]
 
-        def tok_up(b):
+        def tok_up(b, d, col):
             return [
-                remote(tok.at[x, b], tok.at[x, b], tus.at[b], tur.at[b], expert=above),
-                remote(fac.at[x, b], fac.at[x, b], fus.at[b], fur.at[b], expert=above),
+                remote(tok.at[col, b], tok.at[col, b], tus.at[b, d], tur.at[b, d], expert=above),
+                remote(fac.at[col, b], fac.at[col, b], fus.at[b, d], fur.at[b, d], expert=above),
             ]
 
-        def tok_dn(b):
+        def tok_dn(b, d, col):
             return [
-                remote(tok.at[x, b], tok.at[x, b], tds.at[b], tdr.at[b], expert=below),
-                remote(fac.at[x, b], fac.at[x, b], fds.at[b], fdr.at[b], expert=below),
+                remote(tok.at[col, b], tok.at[col, b], tds.at[b, d], tdr.at[b, d], expert=below),
+                remote(fac.at[col, b], fac.at[col, b], fds.at[b, d], fdr.at[b, d], expert=below),
             ]
 
-        def tok_x(d, b, col):
+        def tok_x(d, col):
             to = lax.rem(x + d, nx)
             return [
-                remote(tok.at[col, b], tok.at[col, b], txs.at[d - 1, b], txr.at[d - 1, b], node=to),
-                remote(fac.at[col, b], fac.at[col, b], fxs.at[d - 1, b], fxr.at[d - 1, b], node=to),
+                remote(tok.at[col, z], tok.at[col, z], txs.at[d - 1], txr.at[d - 1], node=to),
+                remote(fac.at[col, z], fac.at[col, z], fxs.at[d - 1], fxr.at[d - 1], node=to),
             ]
 
         tok[x, z] = tokens[...]
         fac[x, z] = factors[...]
+        for d in range(1, nx):
+            for c in tok_x(d, x):
+                c.start()
 
         def tok_step(s, carry):
             bu, bd = z - s, z + s
-
-            @pl.when(bu >= 0)
-            def _():
-                @pl.when(s > 0)
-                def _():
-                    for c in tok_up(bu):
-                        c.wait_recv()
-
-                @pl.when(z < nz - 1)
-                def _():
-                    for c in tok_up(bu):
-                        c.start()
-
-                for d in range(1, nx):
-                    for c in tok_x(d, bu, x):
-                        c.start()
-
-            @pl.when(bd < nz)
-            def _():
-                @pl.when(s > 0)
-                def _():
-                    for c in tok_dn(bd):
-                        c.wait_recv()
-
-                @pl.when(z > 0)
-                def _():
-                    for c in tok_dn(bd):
-                        c.start()
-
-                @pl.when(s > 0)
-                def _():
-                    for d in range(1, nx):
-                        for c in tok_x(d, bd, x):
+            for d in range(nx):
+                col = lax.rem(x + nx - d, nx)
+
+                @pl.when(bu >= 0)
+                def _():
+                    @pl.when(s > 0)
+                    def _():
+                        for c in tok_up(bu, d, col):
+                            c.wait_recv()
+
+                    if d > 0:
+                        @pl.when(s == 0)
+                        def _():
+                            for c in tok_x(d, col):
+                                c.wait_recv()
+
+                    @pl.when(z < nz - 1)
+                    def _():
+                        for c in tok_up(bu, d, col):
+                            c.start()
+
+                @pl.when(bd < nz)
+                def _():
+                    @pl.when(s > 0)
+                    def _():
+                        for c in tok_dn(bd, d, col):
+                            c.wait_recv()
+
+                    @pl.when(z > 0)
+                    def _():
+                        for c in tok_dn(bd, d, col):
                             c.start()
 
             return carry
@@ -312,9 +313,9 @@
         to = lax.rem(i + d, ni)
         return remote(peer_out.at[d - 1, k], out.at[0, k, out_rows()], ps.at[d - 1, k], pr.at[d - 1, k], inner=to)
 
-    def finish_hot():
+    def finish_hot(kinds):
         codes = [jnp.max(meta_i[d - 1, 1:2, :]) for d in range(1, ni)]
-        for k in range(KINDS):
+        for k in kinds:
             for d in range(1, ng):
                 q = lax.rem(g + ng - d, ng)
                 for p in range(nx):
@@ -438,17 +439,15 @@
             def sends(b, carry):
                 @pl.when((b <= z) & (z < nz - 1))
                 def _():
-                    for c in tok_up(b):
-                        c.wait_send()
+                    for d in range(nx):
+                        for c in tok_up(b, d, lax.rem(x + nx - d, nx)):
+                            c.wait_send()
 
                 @pl.when((b >= z) & (z > 0))
                 def _():
-                    for c in tok_dn(b):
-                        c.wait_send()
-
-                for d in range(1, nx):
-                    for c in tok_x(d, b, x):
-                        c.wait_send()
+                    for d in range(nx):
+                        for c in tok_dn(b, d, lax.rem(x + nx - d, nx)):
+                            c.wait_send()
 
                 @pl.when(b > z)
                 def _():
@@ -463,29 +462,33 @@
             lax.fori_loop(0, nz, sends, 0)
             for d in range(1, nx):
                 res_copy(d).wait_send()
+                for c in tok_x(d, x):
+                    c.wait_send()
 
         start_first()
-        lax.fori_loop(0, nz, tok_step, 0)
     else:
         start_first()
     for copy in meta_copies:
         copy.wait_recv()
     hot_step, hot_count = hot_steps()
     if dense:
-        at_own, at_other, at_sum = (hot_count * n // 14 for n in (2, 5, 10))
-        lax.fori_loop(0, at_own, hot_step, 0)
+        at_own, at_other, at_sum = (hot_count * n // 14 for n in (4, 6, 10))
+
+        def early(s, carry):
+            tok_step(s, carry)
+            return hot_step(s, carry)
+
+        lax.fori_loop(0, nz, early, 0)
+        lax.fori_loop(nz, at_own, hot_step, 0)
         for copy in load_copies:
             copy.wait()
         acc[...] = apply(x)
-        lax.fori_loop(at_own, at_other, hot_step, 0)
+        lax.fori_loop(max(nz, at_own), at_other, hot_step, 0)
         for d in range(1, nx):
             col = lax.rem(x + nx - d, nx)
-            for b in range(nz):
-                for c in tok_x(d, b, col):
-                    c.wait_recv()
             res[d - 1] = apply(col).astype(BF16)
             res_copy(d).start()
-        lax.fori_loop(at_other, at_sum, hot_step, 0)
+        lax.fori_loop(max(nz, at_other), at_sum, hot_step, 0)
         for d in range(1, nx):
             res_copy(d).wait_recv()
             acc[...] = acc[...] + xres[d - 1].astype(F32)
@@ -495,13 +498,15 @@
             return sum_step(s - at_sum, carry)
 
         lax.fori_loop(at_sum, hot_count, both, 0)
+        finish_hot(range(1))
         lax.fori_loop(hot_count - at_sum, 2 * nz - 2, sum_step, 0)
-        finish_hot()
+        finish_hot(range(1, KINDS - 1))
         finish_sum()
+        finish_hot(range(KINDS - 1, KINDS))
         drain_moe()
     else:
         lax.fori_loop(0, hot_count, hot_step, 0)
-        finish_hot()
+        finish_hot(range(KINDS))
     drain()
 
 
@@ -573,8 +578,8 @@
             pltpu.VMEM((dx, nz, tok_rows, width), BF16),
             pltpu.VMEM((nz, tok_rows, width), BF16),
             pltpu.VMEM((nz, tok_rows, width), BF16),
-            dma((nz,)), dma((nz,)), dma((nz,)), dma((nz,)), dma((dx, nz)), dma((dx, nz)),
-            dma((nz,)), dma((nz,)), dma((nz,)), dma((nz,)), dma((dx, nz)), dma((dx, nz)),
+            dma((nz, nx)), dma((nz, nx)), dma((nz, nx)), dma((nz, nx)), dma((dx,)), dma((dx,)),
+            dma((nz, nx)), dma((nz, nx)), dma((nz, nx)), dma((nz, nx)), dma((dx,)), dma((dx,)),
             dma((dx,)), dma((dx,)),
             dma((nz,)), dma((nz,)), dma((nz,)), dma((nz,)),
         ]

time: 129 us -> 135 us (1.047)
  Pallas kernels: 119 us -> 125 us
    pallas_call x1, Pallas kernels: 119 us -> 125 us  [shards(): pl.pallas_call(functools.partial(kernel, sizes, dense), out_shape=outs, i...]
where the time goes in v3:
time: 135 us
  Pallas kernels  125 us (93%)
  local copies, waits for them, and re-layouts  7.26 us (5%)
  other arithmetic  1.4 us (1%)
    pallas_call x1, Pallas kernels, shards(): pl.pallas_call(functools.partial(kernel, sizes, dense), out_shape=outs, i...  125 us
    unnamed x2, local copies, waits for them, and re-layouts  6.66 us

profile of v3, /device:TPU:0, one launch (start us, length us, event | category | flops | bytes accessed | tf_op | source)
XLA Modules:
  0.0 135.0 jit_solution(8900227094407507074)
XLA Ops:
  1.3 0.7 add_select_fusion
  2.0 0.7 convert_multiply_fusion
  2.7 0.6 pad.4.refs_4_
  3.3 125.0 %shard_map.104 = (bf16[64,2048]{1,0:T(8,128)(2,1)}, bf16[1,3,2048,384]{3,2,1,0:T(8,128)(2,1)}) custom-call(bf16[1,3,1024,384]{3,2,1,0:T(8,128)(2,1)} %refs_0_.1, s32[2]{0:T(128)} %refs_1_.1, s32[1]{0:T(128)S(6)} %copy.15.refs_2_, bf16[64,2048]{1,0:T(8,128)(2,1)} %refs_3_.1, f32[8,128]{1,0:T(8,128)} %pad.4.refs_4_, bf16[1,2048,384]{2,1,0:T(8,128)(2,1)} %refs_5_.1, ...), custom_call_target="tpu_custom_call" | custom-call | tf_op jit(solution)/shard_map/pallas_call | solution.py:586
  128.3 1.7 %copy.16 = bf16[64,2048]{1,0:T(8,128)(2,1)} copy(bf16[64,2048]{1,0:T(8,128)(2,1)} %get-tuple-element.4) | data formatting | bytes 524288
  130.0 5.0 %copy.17 = bf16[1,3,2048,384]{3,2,1,0:T(8,128)(2,1)} copy(bf16[1,3,2048,384]{3,2,1,0:T(8,128)(2,1)} %get-tuple-element.5) | data formatting | bytes 9437184
  (1 shorter events, 0.0 us)

commit v4 on v2

--- a/solution.py
+++ b/solution.py
@@ -312,9 +312,9 @@
         to = lax.rem(i + d, ni)
         return remote(peer_out.at[d - 1, k], out.at[0, k, out_rows()], ps.at[d - 1, k], pr.at[d - 1, k], inner=to)
 
-    def finish_hot():
+    def finish_hot(kinds):
         codes = [jnp.max(meta_i[d - 1, 1:2, :]) for d in range(1, ni)]
-        for k in range(KINDS):
+        for k in kinds:
             for d in range(1, ng):
                 q = lax.rem(g + ng - d, ng)
                 for p in range(nx):
@@ -465,19 +465,24 @@
                 res_copy(d).wait_send()
 
         start_first()
-        lax.fori_loop(0, nz, tok_step, 0)
     else:
         start_first()
     for copy in meta_copies:
         copy.wait_recv()
     hot_step, hot_count = hot_steps()
     if dense:
-        at_own, at_other, at_sum = (hot_count * n // 14 for n in (2, 5, 10))
-        lax.fori_loop(0, at_own, hot_step, 0)
+        at_own, at_other, at_sum = (hot_count * n // 14 for n in (4, 6, 10))
+
+        def early(s, carry):
+            tok_step(s, carry)
+            return hot_step(s, carry)
+
+        lax.fori_loop(0, nz, early, 0)
+        lax.fori_loop(nz, at_own, hot_step, 0)
         for copy in load_copies:
             copy.wait()
         acc[...] = apply(x)
-        lax.fori_loop(at_own, at_other, hot_step, 0)
+        lax.fori_loop(max(nz, at_own), at_other, hot_step, 0)
         for d in range(1, nx):
             col = lax.rem(x + nx - d, nx)
             for b in range(nz):
@@ -485,7 +490,7 @@
                     c.wait_recv()
             res[d - 1] = apply(col).astype(BF16)
             res_copy(d).start()
-        lax.fori_loop(at_other, at_sum, hot_step, 0)
+        lax.fori_loop(max(nz, at_other), at_sum, hot_step, 0)
         for d in range(1, nx):
             res_copy(d).wait_recv()
             acc[...] = acc[...] + xres[d - 1].astype(F32)
@@ -496,12 +501,13 @@
 
         lax.fori_loop(at_sum, hot_count, both, 0)
         lax.fori_loop(hot_count - at_sum, 2 * nz - 2, sum_step, 0)
-        finish_hot()
+        finish_hot(range(KINDS - 1))
         finish_sum()
+        finish_hot(range(KINDS - 1, KINDS))
         drain_moe()
     else:
         lax.fori_loop(0, hot_count, hot_step, 0)
-        finish_hot()
+        finish_hot(range(KINDS))
     drain()
 
 

time: 129 us -> 128 us (level)
    pallas_call x1, Pallas kernels: 119 us -> 118 us  [shards(): pl.pallas_call(functools.partial(kernel, sizes, dense), out_shape=outs, i...]
where the time goes in v4:
time: 128 us
  Pallas kernels  118 us (92%)
  local copies, waits for them, and re-layouts  7.26 us (6%)
  other arithmetic  1.4 us (1%)
  between operations  1.29 us (1%)
    pallas_call x1, Pallas kernels, shards(): pl.pallas_call(functools.partial(kernel, sizes, dense), out_shape=outs, i...  118 us
    unnamed x2, local copies, waits for them, and re-layouts  6.66 us

profile of v4, /device:TPU:0, one launch (start us, length us, event | category | flops | bytes accessed | tf_op | source)
XLA Modules:
  0.0 127.6 jit_solution(15315039375996746097)
XLA Ops:
  1.3 0.7 add_select_fusion
  2.0 0.7 convert_multiply_fusion
  2.7 0.6 pad.4.refs_4_
  3.3 117.6 %shard_map.104 = (bf16[64,2048]{1,0:T(8,128)(2,1)}, bf16[1,3,2048,384]{3,2,1,0:T(8,128)(2,1)}) custom-call(bf16[1,3,1024,384]{3,2,1,0:T(8,128)(2,1)} %refs_0_.1, s32[2]{0:T(128)} %refs_1_.1, s32[1]{0:T(128)S(6)} %copy.15.refs_2_, bf16[64,2048]{1,0:T(8,128)(2,1)} %refs_3_.1, f32[8,128]{1,0:T(8,128)} %pad.4.refs_4_, bf16[1,2048,384]{2,1,0:T(8,128)(2,1)} %refs_5_.1, ...), custom_call_target="tpu_custom_call" | custom-call | tf_op jit(solution)/shard_map/pallas_call | solution.py:587
  120.9 1.7 %copy.16 = bf16[64,2048]{1,0:T(8,128)(2,1)} copy(bf16[64,2048]{1,0:T(8,128)(2,1)} %get-tuple-element.4) | data formatting | bytes 524288
  122.6 5.0 %copy.17 = bf16[1,3,2048,384]{3,2,1,0:T(8,128)(2,1)} copy(bf16[1,3,2048,384]{3,2,1,0:T(8,128)(2,1)} %get-tuple-element.5) | data formatting | bytes 9437184
  (1 shorter events, 0.0 us)
